TPU v7x, 256 devices: a whole 4x4x8 slice. The times are simulated.
256 devices in a mesh: batch: 32 (over z_lo, x, core), patch: 8 (over z_hi, y).
Axes of the slice: x: 4, y: 4, z: 8 (z_hi: 2, z_lo: 4; z = z_hi * 4 + z_lo), core: 2. Of those that a mesh axis runs over, the one named last changes fastest.
Arguments:
- timestep: int32 [32], P('batch'), parts along dimension 0, may hold values from 0 to 999
- features: bfloat16 [98304, 640], P(('batch', 'patch')), parts along dimension 0, may hold values from -128 to 128
- hidden: bfloat16 [98304, 640], P(('batch', 'patch')), parts along dimension 0, may hold values from -20 to 20
- stale_hidden: bfloat16 [98304, 640], P(('batch', 'patch')), parts along dimension 0, may hold values from -6 to 6
- gn_gain: float32 [640], replicated, may hold values from 0.1 to 1.9
- gn_shift: float32 [640], replicated, may hold values from -3 to 3
- conv_kernel: bfloat16 [3, 3, 640, 640], replicated, may hold values from -0.078125 to 0.078125
- time_weight: bfloat16 [320, 640], replicated, may hold values from -0.3125 to 0.3125
- wq: bfloat16 [640, 640], replicated, may hold values from -0.355756237 to 0.355756237
- wk: bfloat16 [640, 640], replicated, may hold values from -0.237170825 to 0.237170825
- wv: bfloat16 [640, 640], replicated, may hold values from -0.25 to 0.25
Outputs:
- res_out: bfloat16 [98304, 640], P(('batch', 'patch')), parts along dimension 0
- attn_out: bfloat16 [98304, 640], P(('batch', 'patch')), parts along dimension 0
There are 32 independent parts, one for each index of `batch`. A program takes and returns all parts, laid end to end along the dimension named above; an argument that names none is the same for every part. Nothing has to cross between parts.
All inputs are finite; a program needn't handle non-finite values.
Results may differ from a plain program's by a relative error of at most 0.0072.
Values may be sent and summed in bfloat16 or wider, within the bound.
A program may use at most 128 MiB of HBM per device.

v0:
```python
import math

import jax
import jax.numpy as jnp
from jax import lax
from jax.sharding import PartitionSpec as P

HEADS = 10
HEAD_DIM = 64
GROUPS = 16
W = 128


epsilon = 1e-05
very_negative = -1e30


def padded_2(cells, sides, width):
    for axis, dim in sides:
        count = lax.axis_size(axis)
        ends = count - 1
        head = lax.slice_in_dim(cells, 0, width, axis=dim)
        tail = lax.slice_in_dim(cells, cells.shape[dim] - width, cells.shape[dim], axis=dim)
        cells = jnp.concatenate(
            [
                lax.ppermute(tail, axis, [(i, (i + 1) % count) for i in range(ends)]),
                cells,
                lax.ppermute(head, axis, [((i + 1) % count, i) for i in range(ends)]),
            ],
            axis=dim,
        )
    return cells


def project(source, weight):
    return jnp.dot(source, weight, preferred_element_type=jnp.float32).astype(jnp.bfloat16)


def per_device(
    timestep,
    features,
    hidden,
    stale_hidden,
    gn_gain,
    gn_shift,
    conv_kernel,
    time_weight,
    wq,
    wk,
    wv,
):
    row_count = features.shape[0]
    channels = features.shape[1]
    group_width = channels // GROUPS
    values = features.astype(jnp.float32).reshape(row_count, GROUPS, group_width)
    entry_count = row_count * lax.axis_size("patch") * group_width
    group_mean = lax.psum(jnp.sum(values, axis=(0, 2)), "patch") / entry_count
    centered = values - group_mean[None, :, None]
    variance = lax.psum(jnp.sum(centered * centered, axis=(0, 2)), "patch") / entry_count
    normed = (centered * lax.rsqrt(variance + epsilon)[None, :, None]).reshape(row_count, channels)
    activated = jax.nn.silu(normed * gn_gain[None, :] + gn_shift[None, :]).astype(jnp.bfloat16)
    padded = padded_2(activated, (("patch", 0),), W)
    local_rows = row_count // W
    latent_grid = jnp.pad(padded.reshape(local_rows + 2, W, channels), ((0, 0), (1, 1), (0, 0)))
    running_sum = jnp.zeros((row_count, channels), jnp.float32)
    for row_offset in range(3):
        for col_offset in range(3):
            window = latent_grid[
                row_offset : row_offset + local_rows, col_offset : col_offset + W
            ].reshape(row_count, channels)
            running_sum = running_sum + jnp.dot(
                window, conv_kernel[row_offset, col_offset], preferred_element_type=jnp.float32
            )
    half_size = time_weight.shape[0] // 2
    frequencies = jnp.exp(-math.log(10000.0) * jnp.arange(half_size, dtype=jnp.float32) / half_size)
    angles = timestep.astype(jnp.float32)[0] * frequencies
    time_embed = jax.nn.silu(jnp.concatenate([jnp.cos(angles), jnp.sin(angles)])).astype(
        jnp.bfloat16
    )
    time_shift = jnp.dot(time_embed[None, :], time_weight, preferred_element_type=jnp.float32)
    res_out = (running_sum + time_shift).astype(jnp.bfloat16)
    score_scale = 1.0 / math.sqrt(HEAD_DIM)
    queries = project(hidden, wq).reshape(row_count, HEADS, HEAD_DIM)
    fresh_keys = project(hidden, wk).reshape(row_count, HEADS, HEAD_DIM)
    fresh_values = project(hidden, wv).reshape(row_count, HEADS, HEAD_DIM)
    own_first = lax.axis_index("patch") * row_count

    def update(state_now, key_rows, value_rows, keep_mask):
        row_max, weight_sum, summed = state_now
        scores = (
            jnp.einsum("qhd,khd->hqk", queries, key_rows, preferred_element_type=jnp.float32)
            * score_scale
        )
        scores = jnp.where(keep_mask[None, None, :], scores, very_negative)
        new_max = jnp.maximum(row_max, jnp.max(scores, axis=2))
        factor = jnp.exp(row_max - new_max)
        weights = jnp.where(keep_mask[None, None, :], jnp.exp(scores - new_max[:, :, None]), 0.0)
        weight_sum = weight_sum * factor + jnp.sum(weights, axis=2)
        summed = summed * jnp.transpose(factor)[:, :, None] + jnp.einsum(
            "hqk,khd->qhd",
            weights.astype(jnp.bfloat16),
            value_rows,
            preferred_element_type=jnp.float32,
        )
        return (new_max, weight_sum, summed)

    initial = (
        jnp.full((HEADS, row_count), very_negative, jnp.float32),
        jnp.zeros((HEADS, row_count), jnp.float32),
        jnp.zeros((row_count, HEADS, HEAD_DIM), jnp.float32),
    )
    stale_keys = project(stale_hidden, wk).reshape(row_count, HEADS, HEAD_DIM)
    stale_values = project(stale_hidden, wv).reshape(row_count, HEADS, HEAD_DIM)
    key_rows = lax.all_gather(stale_keys, "patch", axis=0, tiled=True)
    value_rows = lax.all_gather(stale_values, "patch", axis=0, tiled=True)
    key_count = key_rows.shape[0]
    position = jnp.arange(key_count, dtype=jnp.int32)
    keep_mask = (position < own_first) | (position >= own_first + row_count)
    block_size = math.gcd(key_count, 1024)

    def block_step(block_index, inner_state):
        offset = block_index * block_size
        return update(
            inner_state,
            lax.dynamic_slice_in_dim(key_rows, offset, block_size, 0),
            lax.dynamic_slice_in_dim(value_rows, offset, block_size, 0),
            lax.dynamic_slice_in_dim(keep_mask, offset, block_size, 0),
        )

    state_now = lax.fori_loop(0, key_count // block_size, block_step, initial)
    state_now = update(state_now, fresh_keys, fresh_values, jnp.ones((row_count,), jnp.bool_))
    row_max, weight_sum, summed = state_now
    attn_out = (
        (summed / jnp.transpose(weight_sum)[:, :, None])
        .reshape(row_count, channels)
        .astype(jnp.bfloat16)
    )
    return (res_out, attn_out)


def solution(mesh):
    placed = (
        P("batch"),
        P(("batch", "patch"), None),
        P(("batch", "patch"), None),
        P(("batch", "patch"), None),
        P(),
        P(),
        P(),
        P(),
        P(),
        P(),
        P(),
    )
    return jax.shard_map(
        per_device,
        mesh=mesh,
        in_specs=placed,
        out_specs=(P(("batch", "patch"), None), P(("batch", "patch"), None)),
        check_vma=False,
    )
```

profile of v0, /device:TPU:28, one launch (start us, length us, event | category | flops | bytes accessed | tf_op | source)
XLA Modules:
  0.0 327.2 jit_solution(9566911143223426562)
XLA Ops:
  11.0 1.9 convolution_convert_fusion.2
  15.3 24.8 %psum.14 = f32[16]{0:T(128)S(1)} all-reduce(f32[16]{0:T(128)S(1)} %reduce_sum.56), channel_id=1, replica_groups=mesh['batch'=32,'patch'=8] {'patch'}, use_global_device_ids=true, to_apply=%region_2.0 | all-reduce | flops 16 | bytes 128 | tf_op jit(solution)/shard_map/psum | solution.py:57
  40.6 26.5 %psum.15 = f32[16]{0:T(128)S(1)} all-reduce(f32[16]{0:T(128)S(1)} %reduce_sum.59), channel_id=1, replica_groups=mesh['batch'=32,'patch'=8] {'patch'}, use_global_device_ids=true, to_apply=%region_5.6 | all-reduce | flops 16 | bytes 128 | tf_op jit(solution)/shard_map/psum | solution.py:59
  68.5 8.0 %collective-permute-start = (bf16[128,640]{1,0:T(8,128)(2,1)}, bf16[128,640]{1,0:T(8,128)(2,1)S(1)}, u32[]{:S(2)}, u32[]{:S(2)}) collective-permute-start(bf16[128,640]{1,0:T(8,128)(2,1)} %get-tuple-element.215), channel_id=1, source_target_pairs={{0,1},{1,2},{2,3},{3,4},{4,5},{5,6},{6,7},{8,9},{9,10},{10,11},{11... | collective-permute-start | bytes 491528 | tf_op jit(solution)/shard_map/ppermute | solution.py:26
  76.5 1.9 collective-permute-start.1
  79.1 1.8 convolution_convert_fusion.3
  83.2 2.7 convolution_convert_fusion
  85.9 3.5 %multiply_reduce_fusion = (f32[10,384]{1,0:T(8,128)S(1)}, f32[10,384,384]{1,2,0:T(8,128)}) fusion(bf16[384,10,64]{0,2,1:T(8,128)(2,1)S(1)} %bitcast.108, bf16[384,10,64]{0,2,1:T(8,128)(2,1)S(1)} %bitcast.121), kind=kOutput, calls=%fused_computation.27 | convolution fusion | flops 191688960 | bytes 6896640 | tf_op jit(solution)/shard_map/qhd,khd->hqk/dot_general | solution.py:91
  90.9 15.0 %collective-permute-done.1 = bf16[128,640]{1,0:T(8,128)(2,1)S(1)} collective-permute-done((bf16[128,640]{1,0:T(8,128)(2,1)}, bf16[128,640]{1,0:T(8,128)(2,1)S(1)}, u32[]{:S(2)}, u32[]{:S(2)}) %collective-permute-start.1) | collective-permute-done | bytes 163872 | tf_op jit(solution)/shard_map/ppermute | solution.py:28
  106.5 1.9 fusion.61
  116.5 4.7 %all-gather.3.cloned.1.call-done = bf16[3072,10,64]{0,2,1:T(8,128)(2,1)} async-done(((bf16[384,10,64]{0,2,1:T(8,128)(2,1)}), bf16[3072,10,64]{0,2,1:T(8,128)(2,1)}) %all-gather.3.cloned.1.call-update) | async-done | bytes 3932176 | tf_op jit(solution)/shard_map/all_gather | solution.py:114
  121.2 111.3 %all-gather.5.cloned.1.call-done = bf16[3072,10,64]{0,2,1:T(8,128)(2,1)} async-done(((bf16[384,10,64]{0,2,1:T(8,128)(2,1)}), bf16[3072,10,64]{0,2,1:T(8,128)(2,1)}) %all-gather.5.cloned.1.call-update) | async-done | bytes 3932176 | tf_op jit(solution)/shard_map/all_gather | solution.py:115
  232.5 79.0 %while.18 = (s32[]{:T(128)}, f32[10,384]{1,0:T(8,128)S(1)}, f32[10,384]{1,0:T(8,128)S(1)}, f32[384,10,64]{0,2,1:T(8,128)}, pred[3072]{0:T(1024)(128)(4,1)S(1)}, ...) while((s32[]{:T(128)}, f32[10,384]{1,0:T(8,128)S(1)}, ...), condition=%wide.region_9.10_spmd.clone, body=%wide.region_6.9_spmd.clone.sunk | while | flops 1058511360 | bytes 115450072 | solution.py:130
  232.5 10.8 %bitcast_reduce_fusion.2 = (f32[10,384]{1,0:T(8,128)S(1)}, f32[10,1024,384]{2,1,0:T(8,128)}) fusion(pred[1024]{0:T(1024)(128)(4,1)S(1)} %dynamic_slice.35, bf16[384,10,64]{0,2,1:T(8,128)(2,1)S(1)} %get-tuple-element.308, bf16[3072,10,64]{0,2,1:T(8,128)(2,1)} %get-tuple-element.307, s32[]{:T(128)S(6)} %select_n.69), kind=kOutput, calls=%fused_computation.1.clone.1 | convolution fusion | flops 515109120 | bytes 17547268 | tf_op jit(solution)/shard_map/while/body/eval_jaxpr/qhd,khd->hqk/dot_general | solution.py:91
  243.3 9.4 %fusion.119 = f32[384,10,64]{0,2,1:T(8,128)} fusion(f32[10,1024,384]{2,1,0:T(8,128)} %get-tuple-element.276, f32[10,384]{1,0:T(8,128)S(1)} %get-tuple-element.303, pred[1024]{0:T(1024)(128)(4,1)S(1)} %dynamic_slice.35, bf16[3072,10,64]{0,2,1:T(8,128)(2,1)} %get-tuple-element.309, s32[]{:T(128)S(6)} %select_n.69, ...), kind=kOutput, calls=%fused_computation.11.clone.1 | convolution fusion | flops 523714560 | bytes 19056644 | tf_op jit(solution)/shard_map/while/body/eval_jaxpr/hqk,khd->qhd/dot_general | solution.py:99
  254.0 4.5 %fusion.117 = f32[10,384]{1,0:T(8,128)S(1)} fusion(f32[10,1024,384]{2,1,0:T(8,128)S(1)} %copy-done.1, f32[10,384]{1,0:T(8,128)S(1)} %get-tuple-element.303, pred[1024]{0:T(1024)(128)(4,1)S(1)} %dynamic_slice.35), kind=kLoop, calls=%fused_computation.6.clone.1 | loop fusion | flops 19656960 | bytes 15760384 | tf_op jit(solution)/shard_map/while/body/eval_jaxpr/reduce_sum | solution.py:98
  258.6 10.8 %bitcast_reduce_fusion.2 = (f32[10,384]{1,0:T(8,128)S(1)}, f32[10,1024,384]{2,1,0:T(8,128)}) fusion(pred[1024]{0:T(1024)(128)(4,1)S(1)} %dynamic_slice.35, bf16[384,10,64]{0,2,1:T(8,128)(2,1)S(1)} %get-tuple-element.308, bf16[3072,10,64]{0,2,1:T(8,128)(2,1)} %get-tuple-element.307, s32[]{:T(128)S(6)} %select_n.69), kind=kOutput, calls=%fused_computation.1.clone.1 | convolution fusion | flops 515109120 | bytes 17547268 | tf_op jit(solution)/shard_map/while/body/eval_jaxpr/qhd,khd->hqk/dot_general | solution.py:91
  269.5 9.7 %fusion.119 = f32[384,10,64]{0,2,1:T(8,128)} fusion(f32[10,1024,384]{2,1,0:T(8,128)} %get-tuple-element.276, f32[10,384]{1,0:T(8,128)S(1)} %get-tuple-element.303, pred[1024]{0:T(1024)(128)(4,1)S(1)} %dynamic_slice.35, bf16[3072,10,64]{0,2,1:T(8,128)(2,1)} %get-tuple-element.309, s32[]{:T(128)S(6)} %select_n.69, ...), kind=kOutput, calls=%fused_computation.11.clone.1 | convolution fusion | flops 523714560 | bytes 19056644 | tf_op jit(solution)/shard_map/while/body/eval_jaxpr/hqk,khd->qhd/dot_general | solution.py:99
  280.5 4.5 %fusion.117 = f32[10,384]{1,0:T(8,128)S(1)} fusion(f32[10,1024,384]{2,1,0:T(8,128)S(1)} %copy-done.1, f32[10,384]{1,0:T(8,128)S(1)} %get-tuple-element.303, pred[1024]{0:T(1024)(128)(4,1)S(1)} %dynamic_slice.35), kind=kLoop, calls=%fused_computation.6.clone.1 | loop fusion | flops 19656960 | bytes 15760384 | tf_op jit(solution)/shard_map/while/body/eval_jaxpr/reduce_sum | solution.py:98
  285.1 10.8 %bitcast_reduce_fusion.2 = (f32[10,384]{1,0:T(8,128)S(1)}, f32[10,1024,384]{2,1,0:T(8,128)}) fusion(pred[1024]{0:T(1024)(128)(4,1)S(1)} %dynamic_slice.35, bf16[384,10,64]{0,2,1:T(8,128)(2,1)S(1)} %get-tuple-element.308, bf16[3072,10,64]{0,2,1:T(8,128)(2,1)} %get-tuple-element.307, s32[]{:T(128)S(6)} %select_n.69), kind=kOutput, calls=%fused_computation.1.clone.1 | convolution fusion | flops 515109120 | bytes 17547268 | tf_op jit(solution)/shard_map/while/body/eval_jaxpr/qhd,khd->hqk/dot_general | solution.py:91
  295.9 9.7 %fusion.119 = f32[384,10,64]{0,2,1:T(8,128)} fusion(f32[10,1024,384]{2,1,0:T(8,128)} %get-tuple-element.276, f32[10,384]{1,0:T(8,128)S(1)} %get-tuple-element.303, pred[1024]{0:T(1024)(128)(4,1)S(1)} %dynamic_slice.35, bf16[3072,10,64]{0,2,1:T(8,128)(2,1)} %get-tuple-element.309, s32[]{:T(128)S(6)} %select_n.69, ...), kind=kOutput, calls=%fused_computation.11.clone.1 | convolution fusion | flops 523714560 | bytes 19056644 | tf_op jit(solution)/shard_map/while/body/eval_jaxpr/hqk,khd->qhd/dot_general | solution.py:99
  306.9 4.5 %fusion.117 = f32[10,384]{1,0:T(8,128)S(1)} fusion(f32[10,1024,384]{2,1,0:T(8,128)S(1)} %copy-done.1, f32[10,384]{1,0:T(8,128)S(1)} %get-tuple-element.303, pred[1024]{0:T(1024)(128)(4,1)S(1)} %dynamic_slice.35), kind=kLoop, calls=%fused_computation.6.clone.1 | loop fusion | flops 19656960 | bytes 15760384 | tf_op jit(solution)/shard_map/while/body/eval_jaxpr/reduce_sum | solution.py:98
  311.5 3.7 %fusion.24 = f32[10,384]{1,0:T(8,128)S(1)} fusion(f32[10,384,384]{1,2,0:T(8,128)} %get-tuple-element.218, f32[10,384]{1,0:T(8,128)S(1)} %get-tuple-element.206), kind=kLoop, calls=%fused_computation.28 | loop fusion | flops 4419840 | bytes 5928960 | tf_op jit(solution)/shard_map/reduce_sum | solution.py:98
  315.2 4.2 %divide_convert_fusion = bf16[384,10,64]{0,2,1:T(8,128)(2,1)S(1)} fusion(bf16[384,10,64]{0,2,1:T(8,128)(2,1)S(1)} %bitcast.122, f32[10,384,384]{1,2,0:T(8,128)} %get-tuple-element.218, f32[10,384]{1,0:T(8,128)S(1)} %get-tuple-element.206, f32[384,10,64]{0,2,1:T(8,128)} %get-tuple-element.143, f32[384,10]{0,1:T(8,128)S(1)} %add_bitcast_fusion, ...), kind=kOutput, calls=%fused_computation.64 | convolution fusion | flops 194150400 | bytes 7910400 | tf_op jit(solution)/shard_map/hqk,khd->qhd/dot_general | solution.py:99
  (82 shorter events, 25.2 us)
Async XLA Ops:
  7.2 1.2 copy-start
  7.2 33.1 %copy-start.2 = (bf16[384,640]{1,0:T(8,128)(2,1)S(1)}, bf16[384,640]{1,0:T(8,128)(2,1)}, u32[]{:S(2)}) copy-start(bf16[384,640]{1,0:T(8,128)(2,1)} %param.14) | copy-start | bytes 1474564
  7.2 60.2 %copy-start.5 = (f32[640]{0:T(1024)S(1)}, f32[640]{0:T(1024)}, u32[]{:S(2)}) copy-start(f32[640]{0:T(1024)} %param.17) | copy-start | bytes 7684
  7.2 60.2 %copy-start.4 = (f32[640]{0:T(1024)S(1)}, f32[640]{0:T(1024)}, u32[]{:S(2)}) copy-start(f32[640]{0:T(1024)} %param.18) | copy-start | bytes 7684
  7.2 71.9 %copy-start.6 = (bf16[384,640]{1,0:T(8,128)(2,1)S(1)}, bf16[384,640]{1,0:T(8,128)(2,1)}, u32[]{:S(2)}) copy-start(bf16[384,640]{1,0:T(8,128)(2,1)} %param.15) | copy-start | bytes 1474564
  7.2 114.0 %all-gather.3.cloned.1.call-start = ((), (), s32[]{:S(2)}) async-start(), calls=%async_computation | async-start | bytes 4423680 | tf_op jit(solution)/shard_map/all_gather | solution.py:114
  11.0 221.5 %all-gather.5.cloned.1.call-start = ((), (), s32[]{:S(2)}) async-start(), calls=%async_computation.1 | async-start | bytes 4423680 | tf_op jit(solution)/shard_map/all_gather | solution.py:115
  68.5 22.4 %collective-permute-start = (bf16[128,640]{1,0:T(8,128)(2,1)}, bf16[128,640]{1,0:T(8,128)(2,1)S(1)}, u32[]{:S(2)}, u32[]{:S(2)}) collective-permute-start(bf16[128,640]{1,0:T(8,128)(2,1)} %get-tuple-element.215), channel_id=1, source_target_pairs={{0,1},{1,2},{2,3},{3,4},{4,5},{5,6},{6,7},{8,9},{9,10},{10,11},{11... | collective-permute-start | bytes 491528 | tf_op jit(solution)/shard_map/ppermute | solution.py:26
  76.5 29.4 %collective-permute-start.1 = (bf16[128,640]{1,0:T(8,128)(2,1)}, bf16[128,640]{1,0:T(8,128)(2,1)S(1)}, u32[]{:S(2)}, u32[]{:S(2)}) collective-permute-start(bf16[128,640]{1,0:T(8,128)(2,1)} %get-tuple-element.216), channel_id=1, source_target_pairs={{1,0},{2,1},{3,2},{4,3},{5,4},{6,5},{7,6},{9,8},{10,9},{11,10},{12... | collective-permute-start | bytes 491528 | tf_op jit(solution)/shard_map/ppermute | solution.py:28
  79.1 11.6 %copy-start.3 = (bf16[320,640]{1,0:T(8,128)(2,1)S(1)}, bf16[320,640]{1,0:T(8,128)(2,1)}, u32[]{:S(2)}) copy-start(bf16[320,640]{1,0:T(8,128)(2,1)} %param.20) | copy-start | bytes 1228804
  90.7 21.2 %slice-start = ((s8[7372800]{0:T(1024)(128)(4,1)}), s8[3178496]{0:T(1024)(128)(4,1)S(1)}, s32[]{:S(2)}) async-start(s8[7372800]{0:T(1024)(128)(4,1)} %bitcast.110), calls=%async_computation.2 | async-start | bytes 6356992
  106.5 5.5 %slice-start.1 = ((s8[7372800]{0:T(1024)(128)(4,1)}), s8[4194304]{0:T(1024)(128)(4,1)S(1)}, s32[]{:S(2)}) async-start(s8[7372800]{0:T(1024)(128)(4,1)} %bitcast.110), calls=%async_computation.3 | async-start | bytes 8388608
  243.3 10.7 %copy-start.1 = (f32[10,1024,384]{2,1,0:T(8,128)S(1)}, f32[10,1024,384]{2,1,0:T(8,128)}, u32[]{:S(2)}) copy-start(f32[10,1024,384]{2,1,0:T(8,128)} %get-tuple-element.276) | copy-start | bytes 47185924 | tf_op jit(solution)/shard_map/while
  269.5 11.0 %copy-start.1 = (f32[10,1024,384]{2,1,0:T(8,128)S(1)}, f32[10,1024,384]{2,1,0:T(8,128)}, u32[]{:S(2)}) copy-start(f32[10,1024,384]{2,1,0:T(8,128)} %get-tuple-element.276) | copy-start | bytes 47185924 | tf_op jit(solution)/shard_map/while
  295.9 11.0 %copy-start.1 = (f32[10,1024,384]{2,1,0:T(8,128)S(1)}, f32[10,1024,384]{2,1,0:T(8,128)}, u32[]{:S(2)}) copy-start(f32[10,1024,384]{2,1,0:T(8,128)} %get-tuple-element.276) | copy-start | bytes 47185924 | tf_op jit(solution)/shard_map/while
Sparse Core Ops, SparseCore 0:
  11.1 110.0 all-gather.2
  123.7 108.7 all-gather.4
where the time goes:
time: 328 us; the launch traced here: 327 us
  waiting for transfers between devices  131 us (40%)
  matrix products  88.7 us (27%)
  blocking collectives  51.3 us (16%)
  other arithmetic  19.5 us (6%)
  between operations  15 us (5%)
  local copies, waits for them, and re-layouts  11.5 us (4%)
  starting transfers between devices  10 us (3%)
    all_gather x1, waiting for transfers between devices, per_device(): value_rows = lax.all_gather(stale_values, 'patch', axis=0, tiled=True)  111 us
    dot_general x4, matrix products, update(): jnp.einsum('qhd,khd->hqk', queries, key_rows, preferred_element_type=jnp....  36 us
    dot_general x4, matrix products, update(): jnp.einsum('hqk,khd->qhd', weights.astype(jnp.bfloat16), value_rows, pref...  33 us
    psum x1, blocking collectives, per_device(): lax.psum(jnp.sum(centered * centered, axis=(0, 2)), 'patch') / entry_count  26.5 us
    psum x1, blocking collectives, per_device(): group_mean = lax.psum(jnp.sum(values, axis=(0, 2)), 'patch') / entry_count  24.8 us
    reduce_sum x4, other arithmetic, update(): weight_sum = weight_sum * factor + jnp.sum(weights, axis=2)  17.2 us
    ppermute x1, waiting for transfers between devices, padded_2(): lax.ppermute(head, axis, [((i + 1) % count, i) for i in range(ends)])  15 us
    dot_general x9, matrix products, per_device(): jnp.dot(window, conv_kernel[row_offset, col_offset], preferred_element_ty...  9.9 us
  transfers between devices with their start and end apart: 4, of which 3 were waited for; matrix products, arithmetic and copies ran while one was open for 9% of the time, Pallas kernels for 0%

commit v1 on v0

v1 whole, which is shorter than its diff:
```python
import functools
import math

import jax
import jax.numpy as jnp
from jax import lax
from jax.experimental import pallas as pl
from jax.experimental.pallas import tpu as pltpu
from jax.sharding import PartitionSpec as P

F32, BF16 = jnp.float32, jnp.bfloat16
MESH = pl.DeviceIdType.MESH
NT = (((1,), (1,)), ((), ()))
HIGHEST = lax.Precision.HIGHEST
TOK, CH, ROW, HALF = 384, 640, 128, 192
GROUPS, GROUP_CH, PATCHES, RING = 16, 40, 8, 4
PAIRS, PAIR_CH, PAIR_Q = 5, 128, 768
VROWS = 144
EPSILON = 1e-05
S_STAT_R, S_STAT_L, S_STAT_O, S_STAT_P, S_HALO_R, S_HALO_L, S_CORNER = range(7)
S_BULK = 7
N_SENDS = S_BULK + 14
R_STAT_L, R_STAT_R, R_STAT_O, R_STAT_P, R_TOP, R_BOTTOM, R_CORNER = range(7)
D_FEAT, D_HID, D_WQ, D_WK, D_WV, D_TW, D_CONV = range(7)


def kernel(
    timestep, feat_hbm, hid_hbm, stale_hbm, gain, shift, conv_hbm, tw_hbm, wq_hbm, wk_hbm, wv_hbm,
    res_ref, attn_ref,
    keys, feats, corner, stats, wq, wk, wv, wvt, tw, convw, act, qt, kbuf, vt, scores, probs,
    row_max, acc, conv_acc, send_sem, recv_sem, bulk_sem, load_sem,
):
    me = lax.axis_index("patch")
    y, zh = lax.rem(me, RING), lax.div(me, RING)
    right = {"patch": zh * RING + lax.rem(y + 1, RING)}
    left = {"patch": zh * RING + lax.rem(y + RING - 1, RING)}
    partner = {"patch": (1 - zh) * RING + y}

    barrier = pltpu.get_barrier_semaphore()
    for device in (right, left, partner):
        pl.semaphore_signal(barrier, inc=1, device_id=device, device_id_type=MESH)

    loads = [
        (D_FEAT, feat_hbm, feats.at[pl.ds(ROW, TOK)]),
        (D_HID, hid_hbm, keys.at[0]),
        (D_WQ, wq_hbm, wq),
        (D_WK, wk_hbm, wk),
        (D_WV, wv_hbm, wv),
        (D_TW, tw_hbm, tw),
        (D_CONV, conv_hbm, convw),
    ]
    load = {i: pltpu.make_async_copy(src, dst, load_sem.at[i]) for i, src, dst in loads}
    for i, _, _ in loads:
        load[i].start()

    def half(ref, h):
        return ref.at[pl.ds(h * HALF, HALF)]

    def remote(slot, src, dst, recv, device):
        return pltpu.make_async_remote_copy(
            src_ref=src, dst_ref=dst, send_sem=send_sem.at[slot], recv_sem=recv,
            device_id=device, device_id_type=MESH,
        )

    def key_half(step, h):
        return keys.at[step, pl.ds(h * HALF, HALF)]

    def bulk(index, src, step, h, device):
        return remote(S_BULK + index, src, key_half(step, h), bulk_sem.at[step, h], device)

    own = lambda h: half(stale_hbm, h)
    bulks = {
        "own0_r": bulk(0, own(0), 1, 0, right),
        "own1_l": bulk(1, own(1), 1, 1, left),
        "own1_r": bulk(2, own(1), 2, 0, right),
        "own0_l": bulk(3, own(0), 2, 1, left),
        "fwd0_r": bulk(4, key_half(1, 0), 3, 0, right),
        "fwd1_l": bulk(5, key_half(1, 1), 3, 1, left),
        "z0": bulk(6, own(0), 4, 0, partner),
        "z1": bulk(7, own(1), 4, 1, partner),
        "p0_r": bulk(8, key_half(4, 0), 5, 0, right),
        "p0_l": bulk(9, key_half(4, 0), 5, 1, left),
        "p1_r": bulk(10, key_half(4, 1), 6, 0, right),
        "p1_l": bulk(11, key_half(4, 1), 6, 1, left),
        "pf0_r": bulk(12, key_half(5, 0), 7, 0, right),
        "pf1_l": bulk(13, key_half(6, 1), 7, 1, left),
    }

    def wait_half(step, h):
        bulk(0, own(0), step, h, right).wait_recv()

    load[D_FEAT].wait()
    x = feats[pl.ds(ROW, TOK), :].astype(F32)
    mean = jnp.sum(x, axis=0, keepdims=True) * (1.0 / TOK)
    stats[0, 0:1, :] = mean
    stats[0, 1:2, :] = jnp.sum((x - mean) * (x - mean), axis=0, keepdims=True)
    stats[0, 2:8, :] = jnp.zeros((6, CH), F32)

    def stat(slot, src, dst, recv, device):
        return remote(slot, stats.at[src], stats.at[dst], recv_sem.at[recv], device)

    stat_r = stat(S_STAT_R, 0, 1, R_STAT_L, right)
    stat_l = stat(S_STAT_L, 0, 2, R_STAT_R, left)
    stat_o = stat(S_STAT_O, 1, 3, R_STAT_O, right)
    stat_p = stat(S_STAT_P, 4, 5, R_STAT_P, partner)
    halo_r = remote(S_HALO_R, feat_hbm.at[pl.ds(TOK - ROW, ROW)], feats.at[pl.ds(0, ROW)], recv_sem.at[R_TOP], right)
    halo_l = remote(S_HALO_L, feat_hbm.at[pl.ds(0, ROW)], feats.at[pl.ds(ROW + TOK, ROW)], recv_sem.at[R_BOTTOM], left)
    corner_top = remote(S_CORNER, feats.at[pl.ds(0, ROW)], corner, recv_sem.at[R_CORNER], partner)
    corner_bottom = remote(S_CORNER, feats.at[pl.ds(ROW + TOK, ROW)], corner, recv_sem.at[R_CORNER], partner)

    pl.semaphore_wait(barrier, 3)
    stat_r.start()
    stat_l.start()
    halo_r.start()
    halo_l.start()
    bulks["own0_r"].start()
    bulks["own1_l"].start()
    bulks["z0"].start()
    bulks["own1_r"].start()
    bulks["own0_l"].start()

    load[D_HID].wait()
    load[D_WQ].wait()
    query = jnp.dot(keys[0], wq[...], preferred_element_type=F32).astype(BF16).astype(F32) * 0.125
    zero = jnp.zeros((PAIR_CH // 2, TOK), BF16)
    for p in range(PAIRS):
        t = query[:, PAIR_CH * p : PAIR_CH * (p + 1)].T.astype(BF16)
        qt[p, 0:64, 0:TOK] = t[0:64]
        qt[p, 64:128, 0:TOK] = zero
        qt[p, 0:64, TOK:PAIR_Q] = zero
        qt[p, 64:128, TOK:PAIR_Q] = t[64:128]
        vt[p, PAIR_CH:VROWS, :] = jnp.ones((VROWS - PAIR_CH, TOK), BF16)
    load[D_WV].wait()
    wvt[...] = wv[...].astype(F32).T.astype(BF16)
    load[D_WK].wait()
    row_max[...] = jnp.full(row_max.shape, -1e30, F32)
    acc[...] = jnp.zeros(acc.shape, F32)

    def attend(step):
        source = keys[step]
        kbuf[...] = jnp.dot(source, wk[...], preferred_element_type=F32).astype(BF16)
        value = lax.dot_general(wvt[...], source, NT, preferred_element_type=F32).astype(BF16)
        for p in range(PAIRS):
            vt[p, 0:PAIR_CH, :] = value[PAIR_CH * p : PAIR_CH * (p + 1), :]

        def score(p):
            scores[p % 2] = jnp.dot(
                kbuf[:, PAIR_CH * p : PAIR_CH * (p + 1)], qt[p], preferred_element_type=F32
            )

        def soften(p):
            s = scores[p % 2]
            old = row_max[p]
            new = jnp.maximum(old, jnp.max(s, axis=0, keepdims=True))
            probs[p % 2] = jnp.exp(s - new).astype(BF16)
            row_max[p] = new
            return jnp.exp(old - new)

        def weigh(p, factor):
            acc[p] = acc[p] * factor + jnp.dot(vt[p], probs[p % 2], preferred_element_type=F32)

        score(0)
        factor = None
        for p in range(PAIRS + 1):
            if p + 1 < PAIRS:
                score(p + 1)
            if p >= 1:
                weigh(p - 1, factor)
            if p < PAIRS:
                factor = soften(p)

    attend(0)

    stat_r.wait_recv()
    stat_l.wait_recv()
    stat_o.start()


    halo_r.wait_recv()
    halo_l.wait_recv()

    @pl.when(me == 0)
    def _():
        corner_top.start()

    @pl.when(me == PATCHES - 1)
    def _():
        corner_bottom.start()

    stat_o.wait_recv()
    s4 = [stats[i] for i in range(4)]
    half_mean = (s4[0] + s4[1] + s4[2] + s4[3]) * 0.25
    half_dev = s4[0] + s4[1] + s4[2] + s4[3]
    spread = sum((s - half_mean) * (s - half_mean) for s in s4) * TOK
    stats[4, 0:1, :] = half_mean[0:1]
    stats[4, 1:2, :] = half_dev[1:2] + spread[0:1]
    stats[4, 2:8, :] = jnp.zeros((6, CH), F32)
    stat_p.start()

    @pl.when((me == RING - 1) | (me == RING))
    def _():
        corner_top.wait_recv()

    @pl.when(me == RING)
    def _():
        feats[pl.ds(0, ROW), :] = corner[...]

    @pl.when(me == RING - 1)
    def _():
        feats[pl.ds(ROW + TOK, ROW), :] = corner[...]

    stat_p.wait_recv()
    a, b = stats[4], stats[5]
    both_mean = (a + b) * 0.5
    channel_dev = (a + b)[1:2] + ((a - b) * (a - b))[0:1] * (TOK * RING * 0.5)
    channel = lax.broadcasted_iota(jnp.int32, (CH, ROW), 0)
    group = lax.broadcasted_iota(jnp.int32, (CH, ROW), 1) * GROUP_CH
    member = ((channel >= group) & (channel < group + GROUP_CH)).astype(F32)

    def over_group(v):
        total = jnp.dot(jnp.broadcast_to(v, (8, CH)), member, precision=HIGHEST, preferred_element_type=F32)
        return lax.dot_general(total, member, NT, precision=HIGHEST, preferred_element_type=F32)[0:1]

    group_mean = over_group(both_mean[0:1]) * (1.0 / GROUP_CH)
    off = both_mean[0:1] - group_mean
    tokens = TOK * PATCHES
    variance = over_group(channel_dev + off * off * tokens) * (1.0 / (GROUP_CH * tokens))
    scale = lax.rsqrt(variance + EPSILON)

    column = lax.broadcasted_iota(jnp.int32, (ROW, CH), 0)
    for r in range(5):
        v = feats[pl.ds(r * ROW, ROW), :].astype(F32)
        v = (v - group_mean) * scale * gain[...] + shift[...]
        v = v / (1.0 + jnp.exp(-v))
        if r == 0:
            v = jnp.where(me == 0, 0.0, v)
        if r == 4:
            v = jnp.where(me == PATCHES - 1, 0.0, v)
        act[pl.ds(r * ROW, ROW), 0:CH] = jnp.where(column == 0, 0.0, pltpu.roll(v, 1, 0)).astype(BF16)
        act[pl.ds(r * ROW, ROW), CH : 2 * CH] = v.astype(BF16)
        act[pl.ds(r * ROW, ROW), 2 * CH : 3 * CH] = jnp.where(
            column == ROW - 1, 0.0, pltpu.roll(v, ROW - 1, 0)
        ).astype(BF16)

    load[D_TW].wait()
    features_half = tw.shape[0] // 2
    j = lax.broadcasted_iota(jnp.int32, (16, features_half), 1).astype(F32)
    angle = timestep[0].astype(F32) * jnp.exp(j * (-math.log(10000.0) / features_half))
    cos, sin = jnp.cos(angle), jnp.sin(angle)
    cos = (cos / (1.0 + jnp.exp(-cos))).astype(BF16)
    sin = (sin / (1.0 + jnp.exp(-sin))).astype(BF16)
    time_shift = jnp.dot(cos, tw[0:features_half, :], preferred_element_type=F32) + jnp.dot(
        sin, tw[features_half:, :], preferred_element_type=F32
    )

    load[D_CONV].wait()
    conv_acc[...] = jnp.broadcast_to(time_shift[0:1], (TOK, CH))

    def conv_row(r, carry):
        conv_acc[...] += jnp.dot(
            act[pl.ds(pl.multiple_of(r * ROW, ROW), TOK), :], convw[r], preferred_element_type=F32
        )
        return carry

    lax.fori_loop(0, 3, conv_row, 0)
    res_ref[...] = conv_acc[...].astype(BF16)

    def stale_step(step, carry):
        @pl.when(step == 3)
        def _():
            wait_half(4, 0)
            bulks["p0_r"].start()
            bulks["p0_l"].start()

        @pl.when(step != 4)
        def _():
            wait_half(step, 0)

        wait_half(step, 1)

        @pl.when(step == 1)
        def _():
            bulks["fwd0_r"].start()
            bulks["fwd1_l"].start()
            bulks["z0"].wait_send()
            bulks["z1"].start()

        @pl.when(step == 4)
        def _():
            bulks["p1_r"].start()
            bulks["p1_l"].start()

        @pl.when(step == 5)
        def _():
            bulks["pf0_r"].start()

        @pl.when(step == 6)
        def _():
            bulks["pf1_l"].start()

        attend(step)
        return carry

    lax.fori_loop(1, PATCHES, stale_step, 0)

    for p in range(PAIRS):
        total = acc[p]
        first = total[0:64, 0:TOK] / total[PAIR_CH : PAIR_CH + 1, 0:TOK]
        second = total[64:128, TOK:PAIR_Q] / total[PAIR_CH : PAIR_CH + 1, TOK:PAIR_Q]
        attn_ref[:, PAIR_CH * p : PAIR_CH * (p + 1)] = jnp.concatenate([first, second], axis=0).T.astype(BF16)

    for copy in (stat_r, stat_l, stat_o, stat_p, halo_r, halo_l):
        copy.wait_send()
    for name, copy in bulks.items():
        if name != "z0":
            copy.wait_send()

    @pl.when((me == 0) | (me == PATCHES - 1))
    def _():
        corner_top.wait_send()


def per_device(timestep, features, hidden, stale_hidden, gn_gain, gn_shift, conv_kernel, time_weight, wq, wk, wv):
    anywhere = pl.BlockSpec(memory_space=pl.ANY)
    vmem = pl.BlockSpec(memory_space=pltpu.VMEM)
    smem = pl.BlockSpec(memory_space=pltpu.SMEM)
    out = jax.ShapeDtypeStruct((TOK, CH), BF16)
    return pl.pallas_call(
        kernel,
        out_shape=(out, out),
        in_specs=[smem, anywhere, anywhere, anywhere, vmem, vmem] + [anywhere] * 5,
        out_specs=(vmem, vmem),
        scratch_shapes=[
            pltpu.VMEM((PATCHES, TOK, CH), BF16),
            pltpu.VMEM((TOK + 2 * ROW, CH), BF16),
            pltpu.VMEM((ROW, CH), BF16),
            pltpu.VMEM((6, 8, CH), F32),
            pltpu.VMEM((CH, CH), BF16),
            pltpu.VMEM((CH, CH), BF16),
            pltpu.VMEM((CH, CH), BF16),
            pltpu.VMEM((CH, CH), BF16),
            pltpu.VMEM((320, CH), BF16),
            pltpu.VMEM((3, 3 * CH, CH), BF16),
            pltpu.VMEM((TOK + 2 * ROW, 3 * CH), BF16),
            pltpu.VMEM((PAIRS, PAIR_CH, PAIR_Q), BF16),
            pltpu.VMEM((TOK, CH), BF16),
            pltpu.VMEM((PAIRS, VROWS, TOK), BF16),
            pltpu.VMEM((2, TOK, PAIR_Q), F32),
            pltpu.VMEM((2, TOK, PAIR_Q), BF16),
            pltpu.VMEM((PAIRS, 1, PAIR_Q), F32),
            pltpu.VMEM((PAIRS, VROWS, PAIR_Q), F32),
            pltpu.VMEM((TOK, CH), F32),
            pltpu.SemaphoreType.DMA((N_SENDS,)),
            pltpu.SemaphoreType.DMA((7,)),
            pltpu.SemaphoreType.DMA((PATCHES, 2)),
            pltpu.SemaphoreType.DMA((7,)),
        ],
        compiler_params=pltpu.CompilerParams(
            collective_id=0, has_side_effects=True, vmem_limit_bytes=56 * 2**20
        ),
    )(
        timestep, features, hidden, stale_hidden, gn_gain.reshape(1, CH), gn_shift.reshape(1, CH),
        conv_kernel.reshape(3, 3 * CH, CH), time_weight, wq, wk, wv,
    )


def solution(mesh):
    tokens = P(("batch", "patch"), None)
    return jax.shard_map(
        per_device,
        mesh=mesh,
        in_specs=(P("batch"), tokens, tokens, tokens) + (P(),) * 7,
        out_specs=(tokens, tokens),
        check_vma=False,
    )
```

time: 328 us -> 74.6 us (0.23)
  waiting for transfers between devices: 131 us -> 0 us
  matrix products: 88.7 us -> 0 us
  Pallas kernels: 0 us -> 65.9 us
  blocking collectives: 51.3 us -> 0 us
  other arithmetic: 19.5 us -> 0 us
  between operations: 15 us -> 1.28 us
  starting transfers between devices: 10 us -> 0 us
  local copies, waits for them, and re-layouts: 11.5 us -> 6.23 us
    all_gather x2 -> x0, waiting for transfers between devices: 116 us -> none  [the longest x1 111 us: per_device(): value_rows = lax.all_gather(stale_values, 'patch', axis=0, tiled=True)]
    dot_general x23 -> x0, matrix products: 88.7 us -> none  [the longest x4 36 us: update(): jnp.einsum('qhd,khd->hqk', queries, key_rows, preferred_element_type=jnp....]
    pallas_call x0 -> x1, Pallas kernels: none -> 65.9 us  [per_device(): pl.pallas_call(kernel, out_shape=(out, out), in_specs=[smem, anywhere, an...]
    psum x2 -> x0, blocking collectives: 51.3 us -> none  [the longest x1 26.5 us: per_device(): lax.psum(jnp.sum(centered * centered, axis=(0, 2)), 'patch') / entry_count]
    reduce_sum x8 -> x0, other arithmetic: 18.8 us -> none  [the longest x4 17.2 us: update(): weight_sum = weight_sum * factor + jnp.sum(weights, axis=2)]
    ppermute x2 -> x0, waiting for transfers between devices: 15 us -> none  [the longest x1 15 us: padded_2(): lax.ppermute(head, axis, [((i + 1) % count, i) for i in range(ends)])]
    ppermute x2 -> x0, starting transfers between devices: 9.94 us -> none  [the longest x1 8.02 us: padded_2(): lax.ppermute(tail, axis, [(i, (i + 1) % count) for i in range(ends)])]
    while x9 -> x0, local copies, waits for them, and re-layouts: 3.83 us -> none
  transfers between devices with their start and end apart: 4 -> 0, of which waited for: 3 -> 0; matrix products, arithmetic and copies ran while one was open for 9% -> 0% of each run, Pallas kernels for 0% -> 0%
where the time goes in v1:
time: 74.6 us; the launch traced here: 73.5 us
  Pallas kernels  65.9 us (88%)
  local copies, waits for them, and re-layouts  6.23 us (8%)
  between operations  1.28 us (2%)
    pallas_call x1, Pallas kernels, per_device(): pl.pallas_call(kernel, out_shape=(out, out), in_specs=[smem, anywhere, an...  65.9 us
    unnamed x2, local copies, waits for them, and re-layouts  3.7 us

profile of v1, /device:TPU:28, one launch (start us, length us, event | category | flops | bytes accessed | tf_op | source)
XLA Modules:
  0.0 73.5 jit_solution(209571711493334479)
XLA Ops:
  1.3 1.3 %reshape.13.gain = f32[1,640]{1,0:T(1,128)} reshape(f32[640]{0:T(1024)} %param.15) | data formatting | bytes 5120 | tf_op jit(solution)/shard_map/reshape | solution.py:362
  2.5 1.3 %reshape.14.shift = f32[1,640]{1,0:T(1,128)} reshape(f32[640]{0:T(1024)} %param.16) | data formatting | bytes 5120 | tf_op jit(solution)/shard_map/reshape | solution.py:362
  3.8 65.9 %shard_map.122 = (bf16[384,640]{1,0:T(8,128)(2,1)}, bf16[384,640]{1,0:T(8,128)(2,1)}) custom-call(s32[1]{0:T(128)S(6)} %copy.15.timestep, bf16[384,640]{1,0:T(8,128)(2,1)} %feat_hbm.1, bf16[384,640]{1,0:T(8,128)(2,1)} %hid_hbm.1, bf16[384,640]{1,0:T(8,128)(2,1)} %stale_hbm.1, f32[1,640]{1,0:T(1,128)} %reshape.13.gain, f32[1,640]{1,0:T(1,128)} %reshape.14.shift, ...), custom_call_target="tpu_custom_call" | custom-call | tf_op jit(solution)/shard_map/pallas_call | solution.py:328
  69.8 1.9 %copy.16 = bf16[384,640]{1,0:T(8,128)(2,1)} copy(bf16[384,640]{1,0:T(8,128)(2,1)} %get-tuple-element.4) | data formatting | bytes 983040
  71.6 1.8 %copy.17 = bf16[384,640]{1,0:T(8,128)(2,1)} copy(bf16[384,640]{1,0:T(8,128)(2,1)} %get-tuple-element.5) | data formatting | bytes 983040

commit v2 on v1

v2 whole, which is shorter than its diff:
```python
import functools
import math

import jax
import jax.numpy as jnp
from jax import lax
from jax.experimental import pallas as pl
from jax.experimental.pallas import tpu as pltpu
from jax.sharding import PartitionSpec as P

F32, BF16 = jnp.float32, jnp.bfloat16
MESH = pl.DeviceIdType.MESH
NT = (((1,), (1,)), ((), ()))
HIGHEST = lax.Precision.HIGHEST
TOK, CH, ROW, HALF, QUARTER, EIGHTH = 384, 640, 128, 192, 96, 48
GROUPS, GROUP_CH, PATCHES, RING = 16, 40, 8, 4
PAIRS, PAIR_CH, PAIR_Q = 5, 128, 768
VROWS = 144
EPSILON = 1e-05
S_STAT_R, S_STAT_L, S_STAT_O, S_STAT_P, S_DOWN, S_UP = range(6)
S_BULK = 6
N_SENDS = S_BULK + 22
R_STAT_L, R_STAT_R, R_STAT_O, R_STAT_P, R_TOP, R_BOTTOM = range(6)
D_FEAT, D_HID, D_WQ, D_WK, D_WV, D_TW, D_CONV, D_GAIN, D_SHIFT, D_STEP = range(10)


def kernel(
    step_hbm, feat_hbm, hid_hbm, stale_hbm, gain_hbm, shift_hbm, conv_hbm, tw_hbm, wq_hbm, wk_hbm, wv_hbm,
    res_ref, attn_ref,
    keys, feats, stats, wq, wk, wv, wvt, tw, convw, act, qt, kbuf, vt, scores, probs,
    row_max, acc, conv_acc, gain, shift, timestep, send_sem, recv_sem, bulk_sem, load_sem, late_sem, seam_sem,
):
    me = lax.axis_index("patch")
    y, zh = lax.rem(me, RING), lax.div(me, RING)
    right = {"patch": zh * RING + lax.rem(y + 1, RING)}
    left = {"patch": zh * RING + lax.rem(y + RING - 1, RING)}
    across = {"patch": zh * RING + lax.rem(y + 2, RING)}
    partner = {"patch": (1 - zh) * RING + y}

    barrier = pltpu.get_barrier_semaphore()
    for device in (right, left, across):
        pl.semaphore_signal(barrier, inc=1, device_id=device, device_id_type=MESH)

    @pl.when(zh == 0)
    def _():
        pl.semaphore_signal(barrier, inc=1, device_id=partner, device_id_type=MESH)

    @pl.when(me == RING - 1)
    def _():
        pl.semaphore_signal(barrier, inc=1, device_id={"patch": me + 1}, device_id_type=MESH)

    loads = [
        (D_FEAT, feat_hbm, feats.at[pl.ds(ROW, TOK)]),
        (D_HID, hid_hbm, keys.at[0]),
        (D_WQ, wq_hbm, wq),
        (D_WK, wk_hbm, wk),
        (D_WV, wv_hbm, wv),
        (D_TW, tw_hbm, tw),
        (D_CONV, conv_hbm, convw),
        (D_GAIN, gain_hbm, gain),
        (D_SHIFT, shift_hbm, shift),
        (D_STEP, step_hbm, timestep),
    ]
    load = {i: pltpu.make_async_copy(src, dst, load_sem.at[i]) for i, src, dst in loads}
    for i, _, _ in loads:
        if i != D_CONV:
            load[i].start()

    def remote(slot, src, dst, recv, device):
        return pltpu.make_async_remote_copy(
            src_ref=src, dst_ref=dst, send_sem=send_sem.at[slot], recv_sem=recv,
            device_id=device, device_id_type=MESH,
        )

    def rows(step, first, count):
        return keys.at[step, pl.ds(first, count)]

    def bulk(index, src, step, first, count, device):
        return remote(
            S_BULK + index, src, rows(step, first, count), bulk_sem.at[step, first // EIGHTH], device
        )

    def own(first, count):
        return stale_hbm.at[pl.ds(first, count)]

    moves = {
        "r0": (own(0, HALF), 1, 0, HALF, right),
        "l1": (own(HALF, HALF), 1, HALF, HALF, left),
        "r1": (own(HALF, HALF), 2, 0, HALF, right),
        "l0": (own(0, HALF), 2, HALF, HALF, left),
        "or": (rows(1, 0, HALF), 3, 0, HALF, right),
        "ol": (rows(1, HALF, HALF), 3, HALF, HALF, left),
        "z0": (own(0, QUARTER), 5, 0, QUARTER, partner),
        "z1": (own(QUARTER, QUARTER), 5, QUARTER, QUARTER, partner),
        "z2": (own(HALF, QUARTER), 5, HALF, QUARTER, partner),
        "z3": (own(HALF + QUARTER, QUARTER), 5, HALF + QUARTER, QUARTER, partner),
        "pr0": (rows(5, 0, HALF), 4, 0, HALF, right),
        "pl0": (rows(5, 0, HALF), 4, HALF, HALF, left),
        "pr2": (rows(5, HALF, QUARTER), 6, HALF, QUARTER, right),
        "pl2": (rows(5, HALF, QUARTER), 6, HALF + QUARTER, QUARTER, left),
        "pr3": (rows(5, HALF + QUARTER, QUARTER), 7, 0, QUARTER, right),
        "pl3": (rows(5, HALF + QUARTER, QUARTER), 7, QUARTER, QUARTER, left),
        "po0": (rows(4, 0, QUARTER), 6, 0, QUARTER, right),
        "po1": (rows(4, HALF + QUARTER, QUARTER), 6, QUARTER, QUARTER, left),
        "po2": (rows(6, HALF, QUARTER), 7, HALF, QUARTER, right),
        "oz": (rows(3, HALF + QUARTER, QUARTER), 7, HALF + QUARTER, QUARTER, partner),
    }
    bulks = {name: bulk(i, *move) for i, (name, move) in enumerate(moves.items())}

    def go(*names):
        for name in names:
            bulks[name].start()

    def got(*names):
        for name in names:
            bulks[name].wait_recv()

    def stat(slot, src, dst, recv, device):
        return remote(slot, stats.at[src], stats.at[dst], recv_sem.at[recv], device)

    stat_r = stat(S_STAT_R, 0, 1, R_STAT_L, right)
    stat_l = stat(S_STAT_L, 0, 2, R_STAT_R, left)
    stat_o = stat(S_STAT_O, 0, 3, R_STAT_O, across)
    stat_p = stat(S_STAT_P, 4, 5, R_STAT_P, partner)
    down = remote(S_DOWN, feat_hbm.at[pl.ds(TOK - ROW, ROW)], feats.at[pl.ds(0, ROW)], recv_sem.at[R_TOP], {"patch": me + 1})
    up = remote(S_UP, feat_hbm.at[pl.ds(0, ROW)], feats.at[pl.ds(ROW + TOK, ROW)], recv_sem.at[R_BOTTOM], {"patch": me - 1})

    @pl.when(me == 0)
    def _():
        feats[pl.ds(0, ROW), :] = jnp.zeros((ROW, CH), BF16)

    @pl.when(me == PATCHES - 1)
    def _():
        feats[pl.ds(ROW + TOK, ROW), :] = jnp.zeros((ROW, CH), BF16)

    def local_stats():
        load[D_FEAT].wait()
        x = feats[pl.ds(ROW, TOK), :].astype(F32)
        mean = jnp.sum(x, axis=0, keepdims=True) * (1.0 / TOK)
        stats[0, 0:1, :] = mean
        stats[0, 1:2, :] = jnp.sum((x - mean) * (x - mean), axis=0, keepdims=True)
        stats[0, 2:8, :] = jnp.zeros((6, CH), F32)

    def prepare():
        load[D_HID].wait()
        load[D_WQ].wait()
        query = jnp.dot(keys[0], wq[...], preferred_element_type=F32).astype(BF16).astype(F32) * 0.125
        zero = jnp.zeros((PAIR_CH // 2, TOK), BF16)
        for p in range(PAIRS):
            t = query[:, PAIR_CH * p : PAIR_CH * (p + 1)].T.astype(BF16)
            qt[p, 0:64, 0:TOK] = t[0:64]
            qt[p, 64:128, 0:TOK] = zero
            qt[p, 0:64, TOK:PAIR_Q] = zero
            qt[p, 64:128, TOK:PAIR_Q] = t[64:128]
            vt[p, PAIR_CH:VROWS, :] = jnp.ones((VROWS - PAIR_CH, TOK), BF16)
        load[D_WV].wait()
        wvt[...] = wv[...].astype(F32).T.astype(BF16)
        load[D_WK].wait()
        row_max[...] = jnp.full(row_max.shape, -1e30, F32)
        acc[...] = jnp.zeros(acc.shape, F32)

    def open_ring():
        @pl.when(zh == 0)
        def _():
            pl.semaphore_wait(barrier, 3)

        @pl.when((zh == 1) & (me != RING))
        def _():
            pl.semaphore_wait(barrier, 4)

        @pl.when(me == RING)
        def _():
            pl.semaphore_wait(barrier, 5)

        stat_r.start()
        stat_l.start()
        stat_o.start()
        go("r0", "l1")

        @pl.when(me == RING)
        def _():
            pl.semaphore_signal(seam_sem, inc=1, device_id={"patch": me - 1}, device_id_type=MESH)
            up.start()

        @pl.when(zh == 1)
        def _():
            pl.semaphore_signal(late_sem, inc=1, device_id=partner, device_id_type=MESH)
            go("z0")

        go("r1", "l0")

        @pl.when((me != RING - 1) & (me < PATCHES - 1))
        def _():
            down.start()

        @pl.when((me != RING) & (me > 0))
        def _():
            up.start()

    early = (zh == 0) & (y < 2)
    local_stats()

    @pl.when(early)
    def _():
        prepare()

    open_ring()

    @pl.when(jnp.logical_not(early))
    def _():
        prepare()

    load[D_CONV].start()

    def attend(step):
        source = keys[step]
        kbuf[...] = jnp.dot(source, wk[...], preferred_element_type=F32).astype(BF16)
        value = lax.dot_general(wvt[...], source, NT, preferred_element_type=F32).astype(BF16)
        for p in range(PAIRS):
            vt[p, 0:PAIR_CH, :] = value[PAIR_CH * p : PAIR_CH * (p + 1), :]

        def score(p):
            scores[p % 2] = jnp.dot(
                kbuf[:, PAIR_CH * p : PAIR_CH * (p + 1)], qt[p], preferred_element_type=F32
            )

        def soften(p):
            s = scores[p % 2]
            old = row_max[p]
            new = jnp.maximum(old, jnp.max(s, axis=0, keepdims=True))
            probs[p % 2] = jnp.exp(s - new).astype(BF16)
            row_max[p] = new
            return jnp.exp(old - new)

        def weigh(p, factor):
            acc[p] = acc[p] * factor + jnp.dot(vt[p], probs[p % 2], preferred_element_type=F32)

        score(0)
        factor = None
        for p in range(PAIRS + 1):
            if p + 1 < PAIRS:
                score(p + 1)
            if p >= 1:
                weigh(p - 1, factor)
            if p < PAIRS:
                factor = soften(p)

    def combine_ring():
        stat_r.wait_recv()
        stat_l.wait_recv()
        stat_o.wait_recv()
        s4 = [stats[i] for i in range(4)]
        half_mean = (s4[0] + s4[1] + s4[2] + s4[3]) * 0.25
        half_dev = s4[0] + s4[1] + s4[2] + s4[3]
        spread = sum((s - half_mean) * (s - half_mean) for s in s4) * TOK
        stats[4, 0:1, :] = half_mean[0:1]
        stats[4, 1:2, :] = half_dev[1:2] + spread[0:1]
        stats[4, 2:8, :] = jnp.zeros((6, CH), F32)

    def resnet():
        @pl.when(me > 0)
        def _():
            down.wait_recv()

        @pl.when(me < PATCHES - 1)
        def _():
            up.wait_recv()

        stat_p.wait_recv()
        a, b = stats[4], stats[5]
        both_mean = (a + b) * 0.5
        channel_dev = (a + b)[1:2] + ((a - b) * (a - b))[0:1] * (TOK * RING * 0.5)
        channel = lax.broadcasted_iota(jnp.int32, (CH, ROW), 0)
        group = lax.broadcasted_iota(jnp.int32, (CH, ROW), 1) * GROUP_CH
        member = ((channel >= group) & (channel < group + GROUP_CH)).astype(F32)

        def over_group(v):
            total = jnp.dot(jnp.broadcast_to(v, (8, CH)), member, precision=HIGHEST, preferred_element_type=F32)
            return lax.dot_general(total, member, NT, precision=HIGHEST, preferred_element_type=F32)[0:1]

        group_mean = over_group(both_mean[0:1]) * (1.0 / GROUP_CH)
        off = both_mean[0:1] - group_mean
        tokens = TOK * PATCHES
        variance = over_group(channel_dev + off * off * tokens) * (1.0 / (GROUP_CH * tokens))
        scale = lax.rsqrt(variance + EPSILON)

        load[D_GAIN].wait()
        load[D_SHIFT].wait()
        gain_row, shift_row = gain[...].reshape(1, CH), shift[...].reshape(1, CH)
        column = lax.broadcasted_iota(jnp.int32, (ROW, CH), 0)
        for r in range(5):
            v = feats[pl.ds(r * ROW, ROW), :].astype(F32)
            v = (v - group_mean) * scale * gain_row + shift_row
            v = v / (1.0 + jnp.exp(-v))
            if r == 0:
                v = jnp.where(me == 0, 0.0, v)
            if r == 4:
                v = jnp.where(me == PATCHES - 1, 0.0, v)
            act[pl.ds(r * ROW, ROW), 0:CH] = jnp.where(column == 0, 0.0, pltpu.roll(v, 1, 0)).astype(BF16)
            act[pl.ds(r * ROW, ROW), CH : 2 * CH] = v.astype(BF16)
            act[pl.ds(r * ROW, ROW), 2 * CH : 3 * CH] = jnp.where(
                column == ROW - 1, 0.0, pltpu.roll(v, ROW - 1, 0)
            ).astype(BF16)

        load[D_TW].wait()
        load[D_STEP].wait()
        features_half = tw.shape[0] // 2
        j = lax.broadcasted_iota(jnp.int32, (16, features_half), 1).astype(F32)
        angle = timestep[0].astype(F32) * jnp.exp(j * (-math.log(10000.0) / features_half))
        cos, sin = jnp.cos(angle), jnp.sin(angle)
        cos = (cos / (1.0 + jnp.exp(-cos))).astype(BF16)
        sin = (sin / (1.0 + jnp.exp(-sin))).astype(BF16)
        time_shift = jnp.dot(cos, tw[0:features_half, :], preferred_element_type=F32) + jnp.dot(
            sin, tw[features_half:, :], preferred_element_type=F32
        )

        load[D_CONV].wait()
        conv_acc[...] = jnp.broadcast_to(time_shift[0:1], (TOK, CH))

        def conv_row(r, carry):
            conv_acc[...] += jnp.dot(
                act[pl.ds(pl.multiple_of(r * ROW, ROW), TOK), :], convw[r], preferred_element_type=F32
            )
            return carry

        conv_row(0, 0)
        got("z0", "z1")
        go("pr0", "pl0")
        lax.fori_loop(1, 3, conv_row, 0)
        res_ref[...] = conv_acc[...].astype(BF16)


    def one_step(step, carry):
        @pl.when(step == 1)
        def _():
            combine_ring()

            @pl.when(zh == 0)
            def _():
                pl.semaphore_wait(late_sem, 1)

            stat_p.start()

            @pl.when(me == RING - 1)
            def _():
                pl.semaphore_wait(seam_sem, 1)
                down.start()

            @pl.when(zh == 0)
            def _():
                go("z0")

            go("z1", "z2", "z3")
            got("r0", "l1")
            go("or", "ol")

        @pl.when(step == 2)
        def _():
            got("r1", "l0")

        @pl.when(step == 3)
        def _():
            resnet()
            got("or", "ol")
            go("oz")

        @pl.when(step == 4)
        def _():
            got("z2")
            go("pr2", "pl2")
            got("pr0", "pl0")
            go("po0", "po1")

        @pl.when(step == 5)
        def _():
            got("z3")
            go("pr3", "pl3")
            got("pr2")
            go("po2")

        @pl.when(step == 6)
        def _():
            got("pl2", "po0", "po1")

        @pl.when(step == 7)
        def _():
            got("pr3", "pl3", "po2", "oz")

        attend(step)
        return carry

    lax.fori_loop(0, PATCHES, one_step, 0)

    for p in range(PAIRS):
        total = acc[p]
        first = total[0:64, 0:TOK] / total[PAIR_CH : PAIR_CH + 1, 0:TOK]
        second = total[64:128, TOK:PAIR_Q] / total[PAIR_CH : PAIR_CH + 1, TOK:PAIR_Q]
        attn_ref[:, PAIR_CH * p : PAIR_CH * (p + 1)] = jnp.concatenate([first, second], axis=0).T.astype(BF16)

    for copy in (stat_r, stat_l, stat_o, stat_p):
        copy.wait_send()

    @pl.when(me < PATCHES - 1)
    def _():
        down.wait_send()

    @pl.when(me > 0)
    def _():
        up.wait_send()

    for copy in bulks.values():
        copy.wait_send()


def per_device(timestep, features, hidden, stale_hidden, gn_gain, gn_shift, conv_kernel, time_weight, wq, wk, wv):
    anywhere = pl.BlockSpec(memory_space=pl.ANY)
    vmem = pl.BlockSpec(memory_space=pltpu.VMEM)
    out = jax.ShapeDtypeStruct((TOK, CH), BF16)
    return pl.pallas_call(
        kernel,
        out_shape=(out, out),
        in_specs=[anywhere] * 11,
        out_specs=(vmem, vmem),
        scratch_shapes=[
            pltpu.VMEM((PATCHES, TOK, CH), BF16),
            pltpu.VMEM((TOK + 2 * ROW, CH), BF16),
            pltpu.VMEM((6, 8, CH), F32),
            pltpu.VMEM((CH, CH), BF16),
            pltpu.VMEM((CH, CH), BF16),
            pltpu.VMEM((CH, CH), BF16),
            pltpu.VMEM((CH, CH), BF16),
            pltpu.VMEM((320, CH), BF16),
            pltpu.VMEM((3, 3 * CH, CH), BF16),
            pltpu.VMEM((TOK + 2 * ROW, 3 * CH), BF16),
            pltpu.VMEM((PAIRS, PAIR_CH, PAIR_Q), BF16),
            pltpu.VMEM((TOK, CH), BF16),
            pltpu.VMEM((PAIRS, VROWS, TOK), BF16),
            pltpu.VMEM((2, TOK, PAIR_Q), F32),
            pltpu.VMEM((2, TOK, PAIR_Q), BF16),
            pltpu.VMEM((PAIRS, 1, PAIR_Q), F32),
            pltpu.VMEM((PAIRS, VROWS, PAIR_Q), F32),
            pltpu.VMEM((TOK, CH), F32),
            pltpu.VMEM((CH,), F32),
            pltpu.VMEM((CH,), F32),
            pltpu.SMEM((1,), jnp.int32),
            pltpu.SemaphoreType.DMA((N_SENDS,)),
            pltpu.SemaphoreType.DMA((6,)),
            pltpu.SemaphoreType.DMA((PATCHES, 8)),
            pltpu.SemaphoreType.DMA((10,)),
            pltpu.SemaphoreType.REGULAR,
            pltpu.SemaphoreType.REGULAR,
        ],
        compiler_params=pltpu.CompilerParams(
            collective_id=0, has_side_effects=True, vmem_limit_bytes=56 * 2**20
        ),
    )(
        timestep, features, hidden, stale_hidden, gn_gain, gn_shift,
        conv_kernel.reshape(3, 3 * CH, CH), time_weight, wq, wk, wv,
    )


def solution(mesh):
    tokens = P(("batch", "patch"), None)
    return jax.shard_map(
        per_device,
        mesh=mesh,
        in_specs=(P("batch"), tokens, tokens, tokens) + (P(),) * 7,
        out_specs=(tokens, tokens),
        check_vma=False,
    )
```

time: 74.6 us -> 63.2 us (0.85)
  the two profiles are of different devices: /device:TPU:28 before, /device:TPU:40 now
where the time goes in v2:
time: 63.2 us; the launch traced here: 63 us
  Pallas kernels  58 us (92%)
  local copies, waits for them, and re-layouts  3.7 us (6%)
  between operations  1.29 us (2%)
    pallas_call x1, Pallas kernels, per_device(): pl.pallas_call(kernel, out_shape=(out, out), in_specs=[anywhere] * 11, ou...  58 us
    unnamed x2, local copies, waits for them, and re-layouts  3.7 us

profile of v2, /device:TPU:40, one launch (start us, length us, event | category | flops | bytes accessed | tf_op | source)
XLA Modules:
  0.0 63.0 jit_solution(13851761218171674026)
XLA Ops:
  1.3 58.0 %shard_map.122 = (bf16[384,640]{1,0:T(8,128)(2,1)}, bf16[384,640]{1,0:T(8,128)(2,1)}) custom-call(s32[1]{0:T(128)S(6)} %copy.15.step_hbm, bf16[384,640]{1,0:T(8,128)(2,1)} %feat_hbm.1, bf16[384,640]{1,0:T(8,128)(2,1)} %hid_hbm.1, bf16[384,640]{1,0:T(8,128)(2,1)} %stale_hbm.1, f32[640]{0:T(1024)} %gain_hbm.1, f32[640]{0:T(1024)} %shift_hbm.1, ...), custom_call_target="tpu_custom_call" | custom-call | tf_op jit(solution)/shard_map/pallas_call | solution.py:419
  59.3 1.9 %copy.16 = bf16[384,640]{1,0:T(8,128)(2,1)} copy(bf16[384,640]{1,0:T(8,128)(2,1)} %get-tuple-element.4) | data formatting | bytes 983040
  61.2 1.8 %copy.17 = bf16[384,640]{1,0:T(8,128)(2,1)} copy(bf16[384,640]{1,0:T(8,128)(2,1)} %get-tuple-element.5) | data formatting | bytes 983040

commit v3 on v2

--- a/solution.py
+++ b/solution.py
@@ -28,7 +28,7 @@
     step_hbm, feat_hbm, hid_hbm, stale_hbm, gain_hbm, shift_hbm, conv_hbm, tw_hbm, wq_hbm, wk_hbm, wv_hbm,
     res_ref, attn_ref,
     keys, feats, stats, wq, wk, wv, wvt, tw, convw, act, qt, kbuf, vt, scores, probs,
-    row_max, acc, conv_acc, gain, shift, timestep, send_sem, recv_sem, bulk_sem, load_sem, late_sem, seam_sem,
+    row_max, acc, conv_acc, norm, gain, shift, timestep, send_sem, recv_sem, bulk_sem, load_sem, late_sem, seam_sem,
 ):
     me = lax.axis_index("patch")
     y, zh = lax.rem(me, RING), lax.div(me, RING)
@@ -180,7 +180,6 @@
         @pl.when(me == RING)
         def _():
             pl.semaphore_signal(seam_sem, inc=1, device_id={"patch": me - 1}, device_id_type=MESH)
-            up.start()
 
         @pl.when(zh == 1)
         def _():
@@ -189,13 +188,6 @@
 
         go("r1", "l0")
 
-        @pl.when((me != RING - 1) & (me < PATCHES - 1))
-        def _():
-            down.start()
-
-        @pl.when((me != RING) & (me > 0))
-        def _():
-            up.start()
 
     early = (zh == 0) & (y < 2)
     local_stats()
@@ -257,15 +249,31 @@
         stats[4, 1:2, :] = half_dev[1:2] + spread[0:1]
         stats[4, 2:8, :] = jnp.zeros((6, CH), F32)
 
-    def resnet():
-        @pl.when(me > 0)
-        def _():
-            down.wait_recv()
-
-        @pl.when(me < PATCHES - 1)
-        def _():
-            up.wait_recv()
-
+    def activate(r):
+        group_mean, scale, gain_row, shift_row = affine_rows()
+        column = lax.broadcasted_iota(jnp.int32, (ROW, CH), 0)
+        v = feats[pl.ds(r * ROW, ROW), :].astype(F32)
+        v = (v - group_mean) * scale * gain_row + shift_row
+        v = v / (1.0 + jnp.exp(-v))
+        if r == 0:
+            v = jnp.where(me == 0, 0.0, v)
+        if r == 4:
+            v = jnp.where(me == PATCHES - 1, 0.0, v)
+        act[pl.ds(r * ROW, ROW), 0:CH] = jnp.where(column == 0, 0.0, pltpu.roll(v, 1, 0)).astype(BF16)
+        act[pl.ds(r * ROW, ROW), CH : 2 * CH] = v.astype(BF16)
+        act[pl.ds(r * ROW, ROW), 2 * CH : 3 * CH] = jnp.where(
+            column == ROW - 1, 0.0, pltpu.roll(v, ROW - 1, 0)
+        ).astype(BF16)
+
+    def affine_rows():
+        return norm[0:1, :], norm[1:2, :], norm[2:3, :], norm[3:4, :]
+
+    def convolve(first_row, first_out, count, tap):
+        conv_acc[pl.ds(first_out, count), :] += jnp.dot(
+            act[pl.ds(first_row, count), :], convw[tap], preferred_element_type=F32
+        )
+
+    def inner_rows():
         stat_p.wait_recv()
         a, b = stats[4], stats[5]
         both_mean = (a + b) * 0.5
@@ -286,21 +294,12 @@
 
         load[D_GAIN].wait()
         load[D_SHIFT].wait()
-        gain_row, shift_row = gain[...].reshape(1, CH), shift[...].reshape(1, CH)
-        column = lax.broadcasted_iota(jnp.int32, (ROW, CH), 0)
-        for r in range(5):
-            v = feats[pl.ds(r * ROW, ROW), :].astype(F32)
-            v = (v - group_mean) * scale * gain_row + shift_row
-            v = v / (1.0 + jnp.exp(-v))
-            if r == 0:
-                v = jnp.where(me == 0, 0.0, v)
-            if r == 4:
-                v = jnp.where(me == PATCHES - 1, 0.0, v)
-            act[pl.ds(r * ROW, ROW), 0:CH] = jnp.where(column == 0, 0.0, pltpu.roll(v, 1, 0)).astype(BF16)
-            act[pl.ds(r * ROW, ROW), CH : 2 * CH] = v.astype(BF16)
-            act[pl.ds(r * ROW, ROW), 2 * CH : 3 * CH] = jnp.where(
-                column == ROW - 1, 0.0, pltpu.roll(v, ROW - 1, 0)
-            ).astype(BF16)
+        norm[0:1, :] = group_mean
+        norm[1:2, :] = scale
+        norm[2:3, :] = gain[...].reshape(1, CH)
+        norm[3:4, :] = shift[...].reshape(1, CH)
+        for r in (1, 2, 3):
+            activate(r)
 
         load[D_TW].wait()
         load[D_STEP].wait()
@@ -316,19 +315,26 @@
 
         load[D_CONV].wait()
         conv_acc[...] = jnp.broadcast_to(time_shift[0:1], (TOK, CH))
-
-        def conv_row(r, carry):
-            conv_acc[...] += jnp.dot(
-                act[pl.ds(pl.multiple_of(r * ROW, ROW), TOK), :], convw[r], preferred_element_type=F32
-            )
-            return carry
-
-        conv_row(0, 0)
+        convolve(ROW, 0, TOK, 1)
         got("z0", "z1")
         go("pr0", "pl0")
-        lax.fori_loop(1, 3, conv_row, 0)
+        convolve(ROW, ROW, 2 * ROW, 0)
+        convolve(2 * ROW, 0, 2 * ROW, 2)
+
+    def outer_rows():
+        @pl.when(me > 0)
+        def _():
+            down.wait_recv()
+
+        @pl.when(me < PATCHES - 1)
+        def _():
+            up.wait_recv()
+
+        activate(0)
+        activate(4)
+        convolve(0, 0, ROW, 0)
+        convolve(4 * ROW, 2 * ROW, ROW, 2)
         res_ref[...] = conv_acc[...].astype(BF16)
-
 
     def one_step(step, carry):
         @pl.when(step == 1)
@@ -341,28 +347,44 @@
 
             stat_p.start()
 
+            @pl.when(zh == 0)
+            def _():
+                go("z0")
+
+            go("z1", "z2", "z3")
+
             @pl.when(me == RING - 1)
             def _():
                 pl.semaphore_wait(seam_sem, 1)
-                down.start()
-
-            @pl.when(zh == 0)
-            def _():
-                go("z0")
-
-            go("z1", "z2", "z3")
+
             got("r0", "l1")
             go("or", "ol")
 
+            @pl.when((me < PATCHES - 1) & (me != RING - 1))
+            def _():
+                down.start()
+
+            @pl.when((me > 0) & (me != RING))
+            def _():
+                up.start()
+
         @pl.when(step == 2)
         def _():
             got("r1", "l0")
 
         @pl.when(step == 3)
         def _():
-            resnet()
+            inner_rows()
             got("or", "ol")
             go("oz")
+
+            @pl.when(me == RING - 1)
+            def _():
+                down.start()
+
+            @pl.when(me == RING)
+            def _():
+                up.start()
 
         @pl.when(step == 4)
         def _():
@@ -384,12 +406,21 @@
 
         @pl.when(step == 7)
         def _():
+            @pl.when((me != RING - 1) & (me != RING))
+            def _():
+                outer_rows()
+
             got("pr3", "pl3", "po2", "oz")
 
         attend(step)
         return carry
 
     lax.fori_loop(0, PATCHES, one_step, 0)
+
+    @pl.when((me == RING - 1) | (me == RING))
+    def _():
+        outer_rows()
+
 
     for p in range(PAIRS):
         total = acc[p]
@@ -408,7 +439,7 @@
     def _():
         up.wait_send()
 
-    for copy in bulks.values():
+    for name, copy in bulks.items():
         copy.wait_send()
 
 
@@ -440,6 +471,7 @@
             pltpu.VMEM((PAIRS, 1, PAIR_Q), F32),
             pltpu.VMEM((PAIRS, VROWS, PAIR_Q), F32),
             pltpu.VMEM((TOK, CH), F32),
+            pltpu.VMEM((8, CH), F32),
             pltpu.VMEM((CH,), F32),
             pltpu.VMEM((CH,), F32),
             pltpu.SMEM((1,), jnp.int32),

time: 63.2 us -> 57.5 us (0.910)
  the two profiles are of different devices: /device:TPU:40 before, /device:TPU:224 now
where the time goes in v3:
time: 57.5 us; the launch traced here: 57.3 us
  Pallas kernels  52.3 us (91%)
  local copies, waits for them, and re-layouts  3.7 us (6%)
  between operations  1.29 us (2%)
    pallas_call x1, Pallas kernels, per_device(): pl.pallas_call(kernel, out_shape=(out, out), in_specs=[anywhere] * 11, ou...  52.3 us
    unnamed x2, local copies, waits for them, and re-layouts  3.7 us

profile of v3, /device:TPU:224, one launch (start us, length us, event | category | flops | bytes accessed | tf_op | source)
XLA Modules:
  0.0 57.3 jit_solution(5921695615768664025)
XLA Ops:
  1.3 52.3 %shard_map.122 = (bf16[384,640]{1,0:T(8,128)(2,1)}, bf16[384,640]{1,0:T(8,128)(2,1)}) custom-call(s32[1]{0:T(128)S(6)} %copy.15.step_hbm, bf16[384,640]{1,0:T(8,128)(2,1)} %feat_hbm.1, bf16[384,640]{1,0:T(8,128)(2,1)} %hid_hbm.1, bf16[384,640]{1,0:T(8,128)(2,1)} %stale_hbm.1, f32[640]{0:T(1024)} %gain_hbm.1, f32[640]{0:T(1024)} %shift_hbm.1, ...), custom_call_target="tpu_custom_call" | custom-call | tf_op jit(solution)/shard_map/pallas_call | solution.py:450
  53.6 1.9 %copy.16 = bf16[384,640]{1,0:T(8,128)(2,1)} copy(bf16[384,640]{1,0:T(8,128)(2,1)} %get-tuple-element.4) | data formatting | bytes 983040
  55.4 1.8 %copy.17 = bf16[384,640]{1,0:T(8,128)(2,1)} copy(bf16[384,640]{1,0:T(8,128)(2,1)} %get-tuple-element.5) | data formatting | bytes 983040

commit v4 on v3

--- a/solution.py
+++ b/solution.py
@@ -321,20 +321,21 @@
         convolve(ROW, ROW, 2 * ROW, 0)
         convolve(2 * ROW, 0, 2 * ROW, 2)
 
-    def outer_rows():
+    def top_row():
         @pl.when(me > 0)
         def _():
             down.wait_recv()
 
+        activate(0)
+        convolve(0, 0, ROW, 0)
+
+    def bottom_row():
         @pl.when(me < PATCHES - 1)
         def _():
             up.wait_recv()
 
-        activate(0)
         activate(4)
-        convolve(0, 0, ROW, 0)
         convolve(4 * ROW, 2 * ROW, ROW, 2)
-        res_ref[...] = conv_acc[...].astype(BF16)
 
     def one_step(step, carry):
         @pl.when(step == 1)
@@ -406,9 +407,13 @@
 
         @pl.when(step == 7)
         def _():
-            @pl.when((me != RING - 1) & (me != RING))
-            def _():
-                outer_rows()
+            @pl.when(me != RING)
+            def _():
+                top_row()
+
+            @pl.when(me != RING - 1)
+            def _():
+                bottom_row()
 
             got("pr3", "pl3", "po2", "oz")
 
@@ -416,10 +421,6 @@
         return carry
 
     lax.fori_loop(0, PATCHES, one_step, 0)
-
-    @pl.when((me == RING - 1) | (me == RING))
-    def _():
-        outer_rows()
 
 
     for p in range(PAIRS):
@@ -428,6 +429,16 @@
         second = total[64:128, TOK:PAIR_Q] / total[PAIR_CH : PAIR_CH + 1, TOK:PAIR_Q]
         attn_ref[:, PAIR_CH * p : PAIR_CH * (p + 1)] = jnp.concatenate([first, second], axis=0).T.astype(BF16)
 
+    @pl.when(me == RING)
+    def _():
+        top_row()
+
+    @pl.when(me == RING - 1)
+    def _():
+        bottom_row()
+
+    res_ref[...] = conv_acc[...].astype(BF16)
+
     for copy in (stat_r, stat_l, stat_o, stat_p):
         copy.wait_send()
 
@@ -441,13 +452,18 @@
 
     for name, copy in bulks.items():
         copy.wait_send()
+
+
+def hand_on(res, attn, res_out, attn_out):
+    res_out[...] = res[...]
+    attn_out[...] = attn[...]
 
 
 def per_device(timestep, features, hidden, stale_hidden, gn_gain, gn_shift, conv_kernel, time_weight, wq, wk, wv):
     anywhere = pl.BlockSpec(memory_space=pl.ANY)
     vmem = pl.BlockSpec(memory_space=pltpu.VMEM)
     out = jax.ShapeDtypeStruct((TOK, CH), BF16)
-    return pl.pallas_call(
+    made = pl.pallas_call(
         kernel,
         out_shape=(out, out),
         in_specs=[anywhere] * 11,
@@ -489,6 +505,12 @@
         timestep, features, hidden, stale_hidden, gn_gain, gn_shift,
         conv_kernel.reshape(3, 3 * CH, CH), time_weight, wq, wk, wv,
     )
+    return pl.pallas_call(
+        hand_on,
+        out_shape=(out, out),
+        in_specs=[vmem, vmem],
+        out_specs=(vmem, vmem),
+    )(*made)
 
 
 def solution(mesh):

time: 57.5 us -> 56 us (0.974)
  the two profiles are of different devices: /device:TPU:224 before, /device:TPU:226 now
where the time goes in v4:
time: 56 us; the launch traced here: 55.9 us
  Pallas kernels  54.6 us (98%)
  between operations  1.29 us (2%)
    pallas_call x1, Pallas kernels, per_device(): pl.pallas_call(kernel, out_shape=(out, out), in_specs=[anywhere] * 11, ou...  52.5 us
    pallas_call x1, Pallas kernels, per_device(): pl.pallas_call(hand_on, out_shape=(out, out), in_specs=[vmem, vmem], out_...  2.16 us

profile of v4, /device:TPU:226, one launch (start us, length us, event | category | flops | bytes accessed | tf_op | source)
XLA Modules:
  0.0 55.9 jit_solution(4403377341054858581)
XLA Ops:
  1.3 52.5 %shard_map.122 = (bf16[384,640]{1,0:T(8,128)(2,1)}, bf16[384,640]{1,0:T(8,128)(2,1)}) custom-call(s32[1]{0:T(128)S(6)} %copy.13.step_hbm, bf16[384,640]{1,0:T(8,128)(2,1)} %feat_hbm.1, bf16[384,640]{1,0:T(8,128)(2,1)} %hid_hbm.1, bf16[384,640]{1,0:T(8,128)(2,1)} %stale_hbm.1, f32[640]{0:T(1024)} %gain_hbm.1, f32[640]{0:T(1024)} %shift_hbm.1, ...), custom_call_target="tpu_custom_call" | custom-call | tf_op jit(solution)/shard_map/pallas_call | solution.py:466
  53.8 2.2 %shard_map.123 = (bf16[384,640]{1,0:T(8,128)(2,1)}, bf16[384,640]{1,0:T(8,128)(2,1)}) custom-call(bf16[384,640]{1,0:T(8,128)(2,1)} %get-tuple-element.4.res, bf16[384,640]{1,0:T(8,128)(2,1)} %get-tuple-element.5.attn), custom_call_target="tpu_custom_call" | custom-call | tf_op jit(solution)/shard_map/pallas_call | solution.py:508

commit v5 on v4

--- a/solution.py
+++ b/solution.py
@@ -17,8 +17,8 @@
 PAIRS, PAIR_CH, PAIR_Q = 5, 128, 768
 VROWS = 144
 EPSILON = 1e-05
-S_STAT_R, S_STAT_L, S_STAT_O, S_STAT_P, S_DOWN, S_UP = range(6)
-S_BULK = 6
+S_STAT_R, S_STAT_L, S_STAT_O, S_STAT_P, S_DOWN, S_UP, S_RELAY = range(7)
+S_BULK = 7
 N_SENDS = S_BULK + 22
 R_STAT_L, R_STAT_R, R_STAT_O, R_STAT_P, R_TOP, R_BOTTOM = range(6)
 D_FEAT, D_HID, D_WQ, D_WK, D_WV, D_TW, D_CONV, D_GAIN, D_SHIFT, D_STEP = range(10)
@@ -28,7 +28,7 @@
     step_hbm, feat_hbm, hid_hbm, stale_hbm, gain_hbm, shift_hbm, conv_hbm, tw_hbm, wq_hbm, wk_hbm, wv_hbm,
     res_ref, attn_ref,
     keys, feats, stats, wq, wk, wv, wvt, tw, convw, act, qt, kbuf, vt, scores, probs,
-    row_max, acc, conv_acc, norm, gain, shift, timestep, send_sem, recv_sem, bulk_sem, load_sem, late_sem, seam_sem,
+    row_max, acc, conv_acc, norm, gain, shift, timestep, send_sem, recv_sem, bulk_sem, load_sem, late_sem,
 ):
     me = lax.axis_index("patch")
     y, zh = lax.rem(me, RING), lax.div(me, RING)
@@ -122,12 +122,9 @@
     stat_l = stat(S_STAT_L, 0, 2, R_STAT_R, left)
     stat_o = stat(S_STAT_O, 0, 3, R_STAT_O, across)
     stat_p = stat(S_STAT_P, 4, 5, R_STAT_P, partner)
-    down = remote(S_DOWN, feat_hbm.at[pl.ds(TOK - ROW, ROW)], feats.at[pl.ds(0, ROW)], recv_sem.at[R_TOP], {"patch": me + 1})
+    down = remote(S_DOWN, feat_hbm.at[pl.ds(TOK - ROW, ROW)], feats.at[pl.ds(0, ROW)], recv_sem.at[R_TOP], right)
+    relay = remote(S_RELAY, feats.at[pl.ds(0, ROW)], feats.at[pl.ds(0, ROW)], recv_sem.at[R_TOP], partner)
     up = remote(S_UP, feat_hbm.at[pl.ds(0, ROW)], feats.at[pl.ds(ROW + TOK, ROW)], recv_sem.at[R_BOTTOM], {"patch": me - 1})
-
-    @pl.when(me == 0)
-    def _():
-        feats[pl.ds(0, ROW), :] = jnp.zeros((ROW, CH), BF16)
 
     @pl.when(me == PATCHES - 1)
     def _():
@@ -177,10 +174,6 @@
         stat_o.start()
         go("r0", "l1")
 
-        @pl.when(me == RING)
-        def _():
-            pl.semaphore_signal(seam_sem, inc=1, device_id={"patch": me - 1}, device_id_type=MESH)
-
         @pl.when(zh == 1)
         def _():
             pl.semaphore_signal(late_sem, inc=1, device_id=partner, device_id_type=MESH)
@@ -354,14 +347,10 @@
 
             go("z1", "z2", "z3")
 
-            @pl.when(me == RING - 1)
-            def _():
-                pl.semaphore_wait(seam_sem, 1)
-
             got("r0", "l1")
             go("or", "ol")
 
-            @pl.when((me < PATCHES - 1) & (me != RING - 1))
+            @pl.when(me < PATCHES - 1)
             def _():
                 down.start()
 
@@ -377,11 +366,14 @@
         def _():
             inner_rows()
             got("or", "ol")
+
+            @pl.when(me == 0)
+            def _():
+                down.wait_recv()
+                relay.start()
+
             go("oz")
 
-            @pl.when(me == RING - 1)
-            def _():
-                down.start()
 
             @pl.when(me == RING)
             def _():
@@ -441,6 +433,10 @@
 
     for copy in (stat_r, stat_l, stat_o, stat_p):
         copy.wait_send()
+
+    @pl.when(me == 0)
+    def _():
+        relay.wait_send()
 
     @pl.when(me < PATCHES - 1)
     def _():
@@ -496,7 +492,6 @@
             pltpu.SemaphoreType.DMA((PATCHES, 8)),
             pltpu.SemaphoreType.DMA((10,)),
             pltpu.SemaphoreType.REGULAR,
-            pltpu.SemaphoreType.REGULAR,
         ],
         compiler_params=pltpu.CompilerParams(
             collective_id=0, has_side_effects=True, vmem_limit_bytes=56 * 2**20

time: 56 us -> 54.3 us (0.970)
  the two profiles are of different devices: /device:TPU:226 before, /device:TPU:28 now
where the time goes in v5:
time: 54.3 us; the launch traced here: 54.2 us
  Pallas kernels  52.9 us (97%)
  between operations  1.29 us (2%)
    pallas_call x1, Pallas kernels, per_device(): pl.pallas_call(kernel, out_shape=(out, out), in_specs=[anywhere] * 11, ou...  50.8 us
    pallas_call x1, Pallas kernels, per_device(): pl.pallas_call(hand_on, out_shape=(out, out), in_specs=[vmem, vmem], out_...  2.16 us

profile of v5, /device:TPU:28, one launch (start us, length us, event | category | flops | bytes accessed | tf_op | source)
XLA Modules:
  0.0 54.2 jit_solution(6371044211302535246)
XLA Ops:
  1.3 50.8 %shard_map.122 = (bf16[384,640]{1,0:T(8,128)(2,1)}, bf16[384,640]{1,0:T(8,128)(2,1)}) custom-call(s32[1]{0:T(128)S(6)} %copy.13.step_hbm, bf16[384,640]{1,0:T(8,128)(2,1)} %feat_hbm.1, bf16[384,640]{1,0:T(8,128)(2,1)} %hid_hbm.1, bf16[384,640]{1,0:T(8,128)(2,1)} %stale_hbm.1, f32[640]{0:T(1024)} %gain_hbm.1, f32[640]{0:T(1024)} %shift_hbm.1, ...), custom_call_target="tpu_custom_call" | custom-call | tf_op jit(solution)/shard_map/pallas_call | solution.py:462
  52.1 2.2 %shard_map.123 = (bf16[384,640]{1,0:T(8,128)(2,1)}, bf16[384,640]{1,0:T(8,128)(2,1)}) custom-call(bf16[384,640]{1,0:T(8,128)(2,1)} %get-tuple-element.4.res, bf16[384,640]{1,0:T(8,128)(2,1)} %get-tuple-element.5.attn), custom_call_target="tpu_custom_call" | custom-call | tf_op jit(solution)/shard_map/pallas_call | solution.py:503

commit v6 on v5

--- a/solution.py
+++ b/solution.py
@@ -17,8 +17,8 @@
 PAIRS, PAIR_CH, PAIR_Q = 5, 128, 768
 VROWS = 144
 EPSILON = 1e-05
-S_STAT_R, S_STAT_L, S_STAT_O, S_STAT_P, S_DOWN, S_UP, S_RELAY = range(7)
-S_BULK = 7
+S_STAT_R, S_STAT_L, S_STAT_O, S_STAT_P, S_DOWN, S_UP, S_RELAY, S_RELAY_UP = range(8)
+S_BULK = 8
 N_SENDS = S_BULK + 22
 R_STAT_L, R_STAT_R, R_STAT_O, R_STAT_P, R_TOP, R_BOTTOM = range(6)
 D_FEAT, D_HID, D_WQ, D_WK, D_WV, D_TW, D_CONV, D_GAIN, D_SHIFT, D_STEP = range(10)
@@ -44,10 +44,6 @@
     @pl.when(zh == 0)
     def _():
         pl.semaphore_signal(barrier, inc=1, device_id=partner, device_id_type=MESH)
-
-    @pl.when(me == RING - 1)
-    def _():
-        pl.semaphore_signal(barrier, inc=1, device_id={"patch": me + 1}, device_id_type=MESH)
 
     loads = [
         (D_FEAT, feat_hbm, feats.at[pl.ds(ROW, TOK)]),
@@ -123,12 +119,9 @@
     stat_o = stat(S_STAT_O, 0, 3, R_STAT_O, across)
     stat_p = stat(S_STAT_P, 4, 5, R_STAT_P, partner)
     down = remote(S_DOWN, feat_hbm.at[pl.ds(TOK - ROW, ROW)], feats.at[pl.ds(0, ROW)], recv_sem.at[R_TOP], right)
+    relay_up = remote(S_RELAY_UP, feats.at[pl.ds(ROW + TOK, ROW)], feats.at[pl.ds(ROW + TOK, ROW)], recv_sem.at[R_BOTTOM], partner)
     relay = remote(S_RELAY, feats.at[pl.ds(0, ROW)], feats.at[pl.ds(0, ROW)], recv_sem.at[R_TOP], partner)
-    up = remote(S_UP, feat_hbm.at[pl.ds(0, ROW)], feats.at[pl.ds(ROW + TOK, ROW)], recv_sem.at[R_BOTTOM], {"patch": me - 1})
-
-    @pl.when(me == PATCHES - 1)
-    def _():
-        feats[pl.ds(ROW + TOK, ROW), :] = jnp.zeros((ROW, CH), BF16)
+    up = remote(S_UP, feat_hbm.at[pl.ds(0, ROW)], feats.at[pl.ds(ROW + TOK, ROW)], recv_sem.at[R_BOTTOM], left)
 
     def local_stats():
         load[D_FEAT].wait()
@@ -161,13 +154,9 @@
         def _():
             pl.semaphore_wait(barrier, 3)
 
-        @pl.when((zh == 1) & (me != RING))
+        @pl.when(zh == 1)
         def _():
             pl.semaphore_wait(barrier, 4)
-
-        @pl.when(me == RING)
-        def _():
-            pl.semaphore_wait(barrier, 5)
 
         stat_r.start()
         stat_l.start()
@@ -354,7 +343,7 @@
             def _():
                 down.start()
 
-            @pl.when((me > 0) & (me != RING))
+            @pl.when(me > 0)
             def _():
                 up.start()
 
@@ -372,12 +361,13 @@
                 down.wait_recv()
                 relay.start()
 
+            @pl.when(me == PATCHES - 1)
+            def _():
+                up.wait_recv()
+                relay_up.start()
+
             go("oz")
 
-
-            @pl.when(me == RING)
-            def _():
-                up.start()
 
         @pl.when(step == 4)
         def _():
@@ -437,6 +427,10 @@
     @pl.when(me == 0)
     def _():
         relay.wait_send()
+
+    @pl.when(me == PATCHES - 1)
+    def _():
+        relay_up.wait_send()
 
     @pl.when(me < PATCHES - 1)
     def _():

time: 54.3 us -> 53.4 us (0.983)
  Pallas kernels: 52.9 us -> 51.7 us
    pallas_call x1, Pallas kernels: 50.8 us -> 49.6 us  [per_device(): pl.pallas_call(kernel, out_shape=(out, out), in_specs=[anywhere] * 11, ou...]
where the time goes in v6:
time: 53.4 us; the launch traced here: 53 us
  Pallas kernels  51.7 us (97%)
  between operations  1.29 us (2%)
    pallas_call x1, Pallas kernels, per_device(): pl.pallas_call(kernel, out_shape=(out, out), in_specs=[anywhere] * 11, ou...  49.6 us
    pallas_call x1, Pallas kernels, per_device(): pl.pallas_call(hand_on, out_shape=(out, out), in_specs=[vmem, vmem], out_...  2.16 us

profile of v6, /device:TPU:28, one launch (start us, length us, event | category | flops | bytes accessed | tf_op | source)
XLA Modules:
  0.0 53.0 jit_solution(15589954365988955748)
XLA Ops:
  1.3 49.6 %shard_map.122 = (bf16[384,640]{1,0:T(8,128)(2,1)}, bf16[384,640]{1,0:T(8,128)(2,1)}) custom-call(s32[1]{0:T(128)S(6)} %copy.13.step_hbm, bf16[384,640]{1,0:T(8,128)(2,1)} %feat_hbm.1, bf16[384,640]{1,0:T(8,128)(2,1)} %hid_hbm.1, bf16[384,640]{1,0:T(8,128)(2,1)} %stale_hbm.1, f32[640]{0:T(1024)} %gain_hbm.1, f32[640]{0:T(1024)} %shift_hbm.1, ...), custom_call_target="tpu_custom_call" | custom-call | tf_op jit(solution)/shard_map/pallas_call | solution.py:456
  50.8 2.2 %shard_map.123 = (bf16[384,640]{1,0:T(8,128)(2,1)}, bf16[384,640]{1,0:T(8,128)(2,1)}) custom-call(bf16[384,640]{1,0:T(8,128)(2,1)} %get-tuple-element.4.res, bf16[384,640]{1,0:T(8,128)(2,1)} %get-tuple-element.5.attn), custom_call_target="tpu_custom_call" | custom-call | tf_op jit(solution)/shard_map/pallas_call | solution.py:497
